TPU v7x, 128 devices: a whole 4x4x4 slice. The times are simulated.
128 devices in a mesh: section: 2 (over core), ctx: 16 (over x, y), tp: 4 (over z).
Axes of the slice: x: 4, y: 4, z: 4, core: 2. Of those that a mesh axis runs over, the one named last changes fastest.
Arguments:
- inputs: bfloat16 [2, 2048, 1024], P(None, 'ctx'), may hold values from -6 to 6
- positions: int32 [2, 2048], P(None, 'ctx'), may hold values from 0 to 1920, as said below
- cotangent: bfloat16 [2, 2048, 1024], P(None, 'ctx'), may hold values from -6 to 6
- attn_gain: bfloat16 [2, 1024], P('section', 'ctx'), may hold values from 0.099609375 to 1.8984375
- w_query: bfloat16 [2, 1024, 2048], P('section', 'ctx', 'tp'), may hold values from -0.1875 to 0.1875
- key_weight_matrix: bfloat16 [2, 1024, 1024], P('section', 'ctx', 'tp'), may hold values from -0.1875 to 0.1875
- value_weight_matrix: bfloat16 [2, 1024, 1024], P('section', 'ctx', 'tp'), may hold values from -0.1875 to 0.1875
- query_gain: bfloat16 [2, 128], P('section'), may hold values from 0.099609375 to 1.8984375
- key_gain: bfloat16 [2, 128], P('section'), may hold values from 0.099609375 to 1.8984375
- w_output: bfloat16 [2, 2048, 1024], P('section', 'tp', 'ctx'), may hold values from -0.75 to 0.75
- mlp_gain: bfloat16 [2, 1024], P('section', 'ctx'), may hold values from 0.099609375 to 1.8984375
- w_gate: bfloat16 [2, 1024, 3072], P('section', 'ctx', 'tp'), may hold values from -0.1875 to 0.1875
- w_up: bfloat16 [2, 1024, 3072], P('section', 'ctx', 'tp'), may hold values from -0.1875 to 0.1875
- w_down: bfloat16 [2, 3072, 1024], P('section', 'tp', 'ctx'), may hold values from -0.109375 to 0.109375
Outputs:
- section_out: bfloat16 [2, 2, 2048, 1024], P('section', None, 'ctx')
- input_grad: float32 [2, 2, 2048, 1024], P('section', None, 'ctx')
- g_attn_gain: float32 [2, 1024], P('section', 'ctx')
- g_query: float32 [2, 1024, 2048], P('section', 'ctx', 'tp')
- g_key: float32 [2, 1024, 1024], P('section', 'ctx', 'tp')
- g_value: float32 [2, 1024, 1024], P('section', 'ctx', 'tp')
- g_query_gain: float32 [2, 128], P('section')
- g_key_gain: float32 [2, 128], P('section')
- g_output: float32 [2, 2048, 1024], P('section', 'tp', 'ctx')
- g_mlp_gain: float32 [2, 1024], P('section', 'ctx')
- g_gate: float32 [2, 1024, 3072], P('section', 'ctx', 'tp')
- g_up: float32 [2, 1024, 3072], P('section', 'ctx', 'tp')
- g_down: float32 [2, 3072, 1024], P('section', 'tp', 'ctx')
Inputs may be any that keep to these rules, and one draw needn't show every extreme that they name: `positions`: positions count the tokens of each packed document from 0 and rise by one from token to token; a document begins where the position is 0. In each micro-batch one document of 1921 tokens begins among the first 128 tokens and ends among the last 128.
All inputs are finite; a program needn't handle non-finite values.
Results may differ from a plain program's by a relative error of at most 0.034.
Values may be sent and summed in bfloat16 or wider, within the bound.
A program may use at most 128 MiB of HBM per device.

v0:
```python
import math

import jax
import jax.numpy as jnp
import numpy as np
from jax import lax
from jax.experimental import pallas as pl
from jax.experimental.pallas import tpu as pltpu
from jax.sharding import PartitionSpec as P

HEAD_SIZE = 128
EPSILON = 1e-06
ROPE_BASE = 1000000.0
MASKED = -1e30
MESH = pl.DeviceIdType.MESH
BF = jnp.bfloat16
F32 = jnp.float32
CTX = 16
TP = 4
ROWS = 128
SUB = ROWS // TP
WIDTH = 1024
BLOCK = WIDTH // CTX
SCALE = 1.0 / math.sqrt(HEAD_SIZE)


def ring(axis, step, count):
    return lax.rem(lax.axis_index(axis) + step, count)


def remote(src, dst, send, recv, **where):
    return pltpu.make_async_remote_copy(
        src_ref=src, dst_ref=dst, send_sem=send, recv_sem=recv, device_id=where, device_id_type=MESH
    )


def params(collective_id, vmem=48):
    return pltpu.CompilerParams(
        collective_id=collective_id, has_side_effects=True, vmem_limit_bytes=vmem * 2**20
    )


VM = pl.BlockSpec(memory_space=pltpu.VMEM)
HB = pl.BlockSpec(memory_space=pl.ANY)
DMA = pltpu.SemaphoreType.DMA


EDGE = 4
HEADS = 4
FIRST = 1280
REST = 2816
GATE, UP, DOWN, OUT = 0, 768, 1536, 2304
GROUPS = ((0, 0, 1280, 384), (1, 2304, 512, 128), (1, 0, 2304, 640))


def place():
    here = lax.axis_index("ctx")
    return here // EDGE, lax.rem(here, EDGE)


def around(value, step):
    return lax.rem(value + step, EDGE)


def peer_x(step):
    x, y = place()
    return around(x, step) * EDGE + y


def peer_y(step):
    x, y = place()
    return x * EDGE + around(y, step)


def greet_plane():
    sem = pltpu.get_barrier_semaphore()
    for step in range(1, EDGE):
        for where in ({"ctx": peer_x(step)}, {"ctx": peer_y(step)}, {"tp": ring("tp", step, TP)}):
            pl.semaphore_signal(sem, inc=1, device_id=where, device_id_type=MESH)
    pl.semaphore_signal(
        sem, inc=1, device_id={"section": 1 - lax.axis_index("section")}, device_id_type=MESH
    )
    pl.semaphore_wait(sem, 3 * (EDGE - 1) + 1)


class PlaneGather:
    def __init__(self, ref, cols_a, cols_b, send, recv):
        self.ref, self.a, self.b, self.send, self.recv = ref, cols_a, cols_b, send, recv
        self.sent = []

    def push(self, src, slot, peer):
        copy = remote(src, src, self.send.at[slot], self.recv.at[slot], ctx=peer)
        copy.start()
        self.sent.append(copy)

    def wait(self, dst, slot):
        remote(dst, dst, self.send.at[slot], self.recv.at[slot], ctx=lax.axis_index("ctx")).wait_recv()

    def start(self):
        x, y = place()
        for step in range(1, EDGE):
            self.push(self.ref.at[x, y, :, self.a], step - 1, peer_x(step))
            self.push(self.ref.at[x, y, :, self.b], step + 2, peer_y(step))

    def middle(self):
        x, y = place()
        for step in range(1, EDGE):
            self.wait(self.ref.at[around(x, EDGE - step), y, :, self.a], step - 1)
        for step in range(1, EDGE):
            self.push(self.ref.at[:, y, :, self.a], step + 5, peer_y(step))
        for step in range(1, EDGE):
            self.wait(self.ref.at[x, around(y, EDGE - step), :, self.b], step + 2)
        for step in range(1, EDGE):
            self.push(self.ref.at[x, :, :, self.b], step + 8, peer_x(step))

    def second(self):
        x, y = place()
        for step in range(1, EDGE):
            yield self.ref.at[:, around(y, EDGE - step), :, self.a], step + 5
            yield self.ref.at[around(x, EDGE - step), :, :, self.b], step + 8

    def end(self):
        for dst, slot in self.second():
            self.wait(dst, slot)

    def finish(self):
        finish(self.sent)


class KeyGather(PlaneGather):
    def start(self):
        x, y = place()
        for step in (1, 3, 2):
            self.push(self.ref.at[x, y, :, self.a], step - 1, peer_x(step))
            self.push(self.ref.at[x, y, :, self.b], step + 14, peer_y(step))
        for step in (1, 3, 2):
            self.push(self.ref.at[x, y, :, self.a], step + 2, peer_y(step))
            self.push(self.ref.at[x, y, :, self.b], step + 17, peer_x(step))

    def middle(self):
        x, y = place()
        for step in (1, 3, 2):
            block = self.ref.at[around(x, EDGE - step), y, :, self.a]
            self.wait(block, step - 1)
            for to in (1, 3, 2):
                self.push(block, 3 * step + to + 2, peer_y(to))
            block = self.ref.at[x, around(y, EDGE - step), :, self.b]
            self.wait(block, step + 14)
            for to in (1, 3, 2):
                self.push(block, 3 * step + to + 17, peer_x(to))

    def end(self):
        x, y = place()
        for to in (1, 3, 2):
            self.wait(self.ref.at[x, around(y, EDGE - to), :, self.a], to + 2)
            self.wait(self.ref.at[around(x, EDGE - to), y, :, self.b], to + 17)
        for step in (1, 3, 2):
            for to in (1, 3, 2):
                self.wait(self.ref.at[around(x, EDGE - step), around(y, EDGE - to), :, self.a], 3 * step + to + 2)
                self.wait(self.ref.at[around(x, EDGE - to), around(y, EDGE - step), :, self.b], 3 * step + to + 17)


class WeightGather(PlaneGather):
    def __init__(self, ref, low, width, first, send, recv, pair_send, pair_recv):
        half = width // 2

        def cols(core):
            start = pl.multiple_of(low + core * half, 128)
            return pl.ds(start, first), pl.ds(pl.multiple_of(start + first, 128), half - first)

        core = lax.axis_index("section")
        super().__init__(ref, *cols(core), send, recv)
        self.theirs = cols(1 - core)
        self.pair_send, self.pair_recv = pair_send, pair_recv

    def hand(self, src, slot):
        other = 1 - lax.axis_index("section")
        copy = remote(src, src, self.pair_send.at[slot], self.pair_recv.at[slot], section=other)
        copy.start()
        self.sent.append(copy)

    def taken(self, dst, slot):
        here = lax.axis_index("section")
        remote(dst, dst, self.pair_send.at[slot], self.pair_recv.at[slot], section=here).wait_recv()

    def middle(self):
        super().middle()
        x, y = place()
        self.hand(self.ref.at[:, y, :, self.a], 0)
        self.hand(self.ref.at[x, :, :, self.b], 1)

    def end(self):
        x, y = place()
        for n, (dst, slot) in enumerate(self.second()):
            self.wait(dst, slot)
            self.hand(dst, n + 2)
        a, b = self.theirs
        self.taken(self.ref.at[:, y, :, a], 0)
        self.taken(self.ref.at[x, :, :, b], 1)
        for step in range(1, EDGE):
            self.taken(self.ref.at[:, around(y, EDGE - step), :, a], 2 * step)
            self.taken(self.ref.at[around(x, EDGE - step), :, :, b], 2 * step + 1)


def mm(a, b, contract=(1, 0)):
    return lax.dot_general(a, b, (((contract[0],), (contract[1],)), ((), ())), preferred_element_type=F32)


def flat(ref, layer, low, size):
    value = ref[layer, :, :, :, low : low + size]
    return value.reshape(-1, size)


def unit_rms(values):
    return values * lax.rsqrt(jnp.mean(values * values, -1, keepdims=True) + EPSILON)


def head(value, index):
    return value[:, index * HEAD_SIZE : (index + 1) * HEAD_SIZE]


def turn(values, gain, cos, sin):
    outs = []
    for index in range(values.shape[1] // HEAD_SIZE):
        scaled = unit_rms(head(values, index)) * gain
        outs.append(scaled * cos + pltpu.roll(scaled, HEAD_SIZE // 2, 1) * sin)
    return jnp.concatenate(outs, 1).astype(BF)


def scores_t(keys, query, first):
    raw = mm(keys, query, (1, 1)) * SCALE
    rows = lax.broadcasted_iota(jnp.int32, raw.shape, 0)
    last = lax.axis_index("ctx") * ROWS + lax.broadcasted_iota(jnp.int32, (1, ROWS), 1)
    return jnp.where((rows <= last) & (rows >= first), raw, MASKED)


def forward_layer(layer, hidden, w1, w2, first, cos, sin, st, tp_sems, keys_gather, groups, following):
    here = lax.axis_index("tp")
    x, y = place()
    rows = pl.ds(pl.multiple_of(here * SUB, SUB), SUB)
    part, landing = st["part"], st["landing"]
    groups[0].end()
    gains = flat(w1, layer, 1024, 128).astype(F32).T[:8]
    st["gains"][layer] = gains
    heads = w1[layer, 0, 0, 0:16, 1152:1280].astype(F32)
    st["head_gains"][layer] = heads[:8]
    normed = (unit_rms(hidden[...].astype(F32)) * gains[0:1]).astype(BF)
    st["normed"][layer] = normed
    key_proj = mm(normed, flat(w1, layer, 512, 256))
    value = mm(normed, flat(w1, layer, 768, 256))
    st["key_proj"][layer] = key_proj
    kv = st["kv"]
    kv[layer, x, y, :, 0:256] = turn(key_proj, heads[1:2], cos, sin)
    kv[layer, x, y, :, 256:512] = value.astype(BF)
    keys_gather.start()
    query_proj = mm(normed, flat(w1, layer, 0, 512))
    st["query_proj"][layer] = query_proj
    query = turn(query_proj, heads[0:1], cos, sin)
    st["query"][layer] = query
    st["keep"](0, layer)
    keys_gather.middle()
    if following:
        groups[1].middle()
    keys_gather.end()
    st["keep"](2, layer)
    groups[2].middle()
    mixed = []
    for group in range(2):
        keys = flat(kv, layer, group * HEAD_SIZE, HEAD_SIZE)
        values_t = flat(kv, layer, 256 + group * HEAD_SIZE, HEAD_SIZE).T
        for index in (2 * group, 2 * group + 1):
            scores = scores_t(keys, head(query, index), first)
            top = jnp.max(scores, 0, keepdims=True)
            raised = jnp.exp(scores - top)
            total = jnp.sum(raised, 0, keepdims=True)
            low = (raised * (1.0 / total)).astype(BF)
            st["level"][layer, index : index + 1, :] = top + jnp.log(total)
            mixed.append(mm(values_t, low).T.astype(BF))
    mixed = jnp.concatenate(mixed, 1)
    st["mixed"][layer] = mixed
    groups[1].end()
    part[2 * layer] = mm(mixed, flat(w2, layer, OUT, 512), (1, 1)).astype(BF)
    sems = [s.at[2 * layer] for s in tp_sems]
    sent = tp_scatter(part.at[2 * layer], landing.at[2 * layer], sems[0], sems[1])
    if following:
        following[0].start()
    total = tp_total(part.at[2 * layer], landing.at[2 * layer], sent)
    after = total + hidden[rows, :].astype(F32)
    st["after"][layer] = after
    mlp_in = st["mlp_in"].at[layer]
    mlp_in[rows, :] = (unit_rms(after) * gains[1:2]).astype(BF)
    sent += tp_spread(mlp_in, sems[2], sems[3])
    if following:
        following[0].middle()
    groups[2].end()
    tp_spread_wait(mlp_in, sems[2], sems[3])
    gate = mm(mlp_in[...], flat(w2, layer, GATE, 768))
    up = mm(mlp_in[...], flat(w2, layer, UP, 768))
    st["gate"][layer] = gate
    st["up"][layer] = up
    activated = (gate / (1.0 + jnp.exp(-gate)) * up).astype(BF)
    st["keep"](1, layer)
    if following:
        for group in following[1:]:
            group.start()
    part[2 * layer + 1] = mm(activated, flat(w2, layer, DOWN, 768), (1, 1)).astype(BF)
    sems = [s.at[2 * layer + 1] for s in tp_sems]
    copies = tp_scatter(part.at[2 * layer + 1], landing.at[2 * layer + 1], sems[0], sems[1])
    total = tp_total(part.at[2 * layer + 1], landing.at[2 * layer + 1], copies)
    out = st["outs"].at[layer]
    out[rows, :] = (total + after).astype(BF)
    copies += tp_spread(out, sems[2], sems[3])
    if following:
        following[1].middle()
    tp_spread_wait(out, sems[2], sems[3])
    return sent + copies


STASH = dict(
    first=((1, ROWS), jnp.int32),
    cos=((ROWS, HEAD_SIZE), F32),
    sin=((ROWS, HEAD_SIZE), F32),
    normed=((2, ROWS, WIDTH), BF),
    query_proj=((2, ROWS, 512), F32),
    key_proj=((2, ROWS, 256), F32),
    query=((2, ROWS, 512), BF),
    level=((2, 8, ROWS), F32),
    mixed=((2, ROWS, 512), BF),
    after=((2, SUB, WIDTH), F32),
    mlp_in=((2, ROWS, WIDTH), BF),
    gate=((2, ROWS, 768), F32),
    up=((2, ROWS, 768), F32),
    outs=((2, ROWS, WIDTH), BF),
    gains=((2, 8, WIDTH), F32),
    head_gains=((2, 8, HEAD_SIZE), F32),
)
KEPT = [
    ((2, EDGE, EDGE, BLOCK, FIRST), BF),
    ((2, EDGE, EDGE, BLOCK, REST), BF),
    ((2, EDGE, EDGE, ROWS, 512), BF),
]


def forward_kernel(
    inputs, positions, attn_gain, w_query, w_key, w_value, query_gain, key_gain, w_output, mlp_gain, w_gate, w_up,
    w_down, speeds, w1_out, w2_out, kv_out, *refs
):
    st = dict(zip(STASH, refs))
    own1, own2, w1, w2, st["kv"], st["part"], st["landing"], *refs = refs[len(STASH) :]
    tp_sems, (local, swap_send, swap_recv, send, recv, pair_send, pair_recv, kv_send, kv_recv, keep) = refs[:4], refs[4:]
    core = lax.axis_index("section")
    other = 1 - core
    x, y = place()
    kept = []

    def keep_copy(n, layer):
        src, dst = ((w1, w1_out), (w2, w2_out), (st["kv"], kv_out))[n]
        kept.append(pltpu.make_async_copy(src.at[layer], dst.at[layer], keep.at[layer, n]))
        kept[-1].start()

    st["keep"] = keep_copy
    gathers = [
        [
            WeightGather((w1, w2)[which].at[layer], low, width, along_x, send.at[layer, n], recv.at[layer, n],
                         pair_send.at[layer, n], pair_recv.at[layer, n])
            for n, (which, low, width, along_x) in enumerate(GROUPS)
        ]
        for layer in range(2)
    ]
    own1[:, 0:512] = w_query[0]
    own1[:, 512:768] = w_key[0]
    own1[:, 768:1024] = w_value[0]
    tail = [attn_gain[...].astype(F32), mlp_gain[...].astype(F32), jnp.zeros((126, BLOCK), F32)]
    own1[:, 1024:1152] = jnp.concatenate(tail, 0).T.astype(BF)
    tail = [query_gain[...].astype(F32), key_gain[...].astype(F32), jnp.zeros((BLOCK - 2, HEAD_SIZE), F32)]
    own1[:, 1152:1280] = jnp.concatenate(tail, 0).astype(BF)
    own2[:, GATE : GATE + 768] = w_gate[0]
    own2[:, UP : UP + 768] = w_up[0]
    own2[:, OUT : OUT + 512] = w_output[0]
    own2[:, DOWN : DOWN + 768] = w_down[0]
    greet_plane()
    swaps, locals_ = [], []
    for n, (own, ref) in enumerate(((own1, w1), (own2, w2))):
        for low, width in [(g[1], g[2]) for g in GROUPS if g[0] == n]:
            slot = len(swaps)
            half = width // 2
            cut = pl.ds(pl.multiple_of(low + other * half, 128), half)
            mine = pl.ds(pl.multiple_of(low + core * half, 128), half)
            swaps.append(
                remote(own.at[:, cut], ref.at[core, x, y, :, cut], swap_send.at[slot], swap_recv.at[slot], section=other)
            )
            swaps[-1].start()
            locals_.append(pltpu.make_async_copy(own.at[:, mine], ref.at[core, x, y, :, mine], local.at[slot]))
            locals_[-1].start()
    for slot, (n, low, width, _) in enumerate(GROUPS):
        half = width // 2
        dst = (w1, w2)[n].at[other, x, y, :, pl.ds(pl.multiple_of(low + core * half, 128), half)]
        locals_[slot].wait()
        remote(dst, dst, swap_send.at[slot], swap_recv.at[slot], section=core).wait_recv()
        if slot == 0:
            gathers[0][0].start()
    gathers[0][0].middle()
    for group in gathers[0][1:]:
        group.start()
    keys = [
        KeyGather(st["kv"].at[layer], pl.ds(0, 256), pl.ds(256, 256), kv_send.at[layer], kv_recv.at[layer])
        for layer in range(2)
    ]
    token_pos = positions[pl.ds(core, 1), :]
    first = lax.axis_index("ctx") * ROWS + lax.broadcasted_iota(jnp.int32, (1, ROWS), 1) - token_pos
    angles = jnp.broadcast_to(token_pos.astype(F32), (ROWS, ROWS)).T * speeds[...]
    cos, sin = jnp.cos(angles), jnp.sin(angles)
    low_half = lax.broadcasted_iota(jnp.int32, (ROWS, HEAD_SIZE), 1) < HEAD_SIZE // 2
    tables = first, cos, jnp.where(low_half, -sin, sin)
    for name, table in zip(("first", "cos", "sin"), tables):
        st[name][...] = table
    sent = forward_layer(0, inputs.at[core], w1, w2, *tables, st, tp_sems, keys[0], gathers[0], gathers[1])
    sent += forward_layer(1, st["outs"].at[0], w1, w2, *tables, st, tp_sems, keys[1], gathers[1], None)
    finish(sent + swaps)
    for part in keys + gathers[0] + gathers[1]:
        part.finish()
    for copy in kept:
        copy.wait()


def run_forward(*args):
    outs = KEPT + list(STASH.values())
    speeds = ROPE_BASE ** (-(np.arange(HEAD_SIZE // 2, dtype=np.float32) * np.float32(2.0 / HEAD_SIZE)))
    speeds = jnp.asarray(np.tile(speeds, 2)[None].astype(np.float32))
    return pl.pallas_call(
        forward_kernel,
        out_shape=[jax.ShapeDtypeStruct(*o) for o in outs],
        in_specs=[VM] * (len(args) + 1),
        out_specs=[HB] * 3 + [VM] * len(STASH),
        scratch_shapes=[
            pltpu.VMEM((BLOCK, FIRST), BF),
            pltpu.VMEM((BLOCK, REST), BF),
            *[pltpu.VMEM(*k) for k in KEPT],
            pltpu.VMEM((4, ROWS, WIDTH), BF),
            pltpu.VMEM((4, TP - 1, SUB, WIDTH), BF),
            *[DMA((4, TP - 1))] * 4,
            DMA((3,)), DMA((3,)), DMA((3,)),
            DMA((2, 3, 12)), DMA((2, 3, 12)), DMA((2, 3, 8)), DMA((2, 3, 8)), DMA((2, 30)), DMA((2, 30)), DMA((2, 3)),
        ],
        compiler_params=params(1, 60),
    )(*args, speeds)


def tp_rows(ref, index):
    return ref.at[pl.ds(pl.multiple_of(index * SUB, SUB), SUB)]


def tp_scatter(part, landing, send, recv):
    copies = []
    for step in range(1, TP):
        peer = ring("tp", step, TP)
        copies.append(
            remote(tp_rows(part, peer), landing.at[step - 1], send.at[step - 1], recv.at[step - 1], tp=peer)
        )
        copies[-1].start()
    return copies


def tp_total(part, landing, copies):
    total = tp_rows(part, lax.axis_index("tp"))[...].astype(F32)
    for step, copy in enumerate(copies):
        copy.wait_recv()
        total = total + landing[step].astype(F32)
    return total


def tp_spread(full, send, recv):
    here = lax.axis_index("tp")
    copies = []
    for step in range(1, TP):
        rows = tp_rows(full, here)
        copies.append(remote(rows, rows, send.at[step - 1], recv.at[step - 1], tp=ring("tp", step, TP)))
        copies[-1].start()
    return copies


def tp_spread_wait(full, send, recv):
    here = lax.axis_index("tp")
    for step in range(TP - 1):
        rows = tp_rows(full, ring("tp", TP - 1 - step, TP))
        remote(rows, rows, send.at[step], recv.at[step], tp=here).wait_recv()


def finish(copies):
    for copy in copies:
        copy.wait_send()


def norm_back(values, grad, gain):
    inverse = lax.rsqrt(jnp.mean(values * values, -1, keepdims=True) + EPSILON)
    unit = values * inverse
    scaled = grad * gain
    back = inverse * (scaled - unit * jnp.mean(scaled * unit, -1, keepdims=True))
    return back, jnp.sum(grad * unit, 0, keepdims=True)


class PlaneScatter:
    def __init__(self, ref, cols_a, cols_b, lands, send, recv):
        self.ref, self.a, self.b, self.send, self.recv = ref, cols_a, cols_b, send, recv
        self.lands = lands
        self.sent = []

    def push(self, src, land, slot, peer):
        copy = remote(src, land, self.send.at[slot], self.recv.at[slot], ctx=peer)
        copy.start()
        self.sent.append(copy)

    def add(self, own, phase, slot):
        land = self.lands[phase]
        for step in range(EDGE - 1):
            dst = land.at[step]
            sems = self.send.at[slot + step], self.recv.at[slot + step]
            remote(dst, dst, *sems, ctx=lax.axis_index("ctx")).wait_recv()
        total = own[...].astype(F32)
        for step in range(EDGE - 1):
            total = total + land[step].astype(F32)
        return total

    def start(self):
        x, y = place()
        for step in range(1, EDGE):
            self.push(self.ref.at[around(x, step), :, :, self.a], self.lands[0].at[step - 1], step - 1, peer_x(step))
            self.push(self.ref.at[:, around(y, step), :, self.b], self.lands[1].at[step - 1], step + 2, peer_y(step))

    def middle(self):
        x, y = place()
        own = self.ref.at[x, :, :, self.a]
        own[...] = self.add(own, 0, 0).astype(BF)
        for step in range(1, EDGE):
            self.push(self.ref.at[x, around(y, step), :, self.a], self.lands[2].at[step - 1], step + 5, peer_y(step))
        own = self.ref.at[:, y, :, self.b]
        own[...] = self.add(own, 1, 3).astype(BF)
        for step in range(1, EDGE):
            self.push(self.ref.at[around(x, step), y, :, self.b], self.lands[3].at[step - 1], step + 8, peer_x(step))

    def end(self):
        x, y = place()
        return self.add(self.ref.at[x, y, :, self.a], 2, 6), self.add(self.ref.at[x, y, :, self.b], 3, 9)

    def finish(self):
        finish(self.sent)


GRAD_HALF = {1024: (256, 256), REST: (768, 640)}


def scatter_lands(rows, first, second):
    return [
        ((EDGE - 1, EDGE, rows, first), BF),
        ((EDGE - 1, EDGE, rows, second), BF),
        ((EDGE - 1, rows, first), BF),
        ((EDGE - 1, rows, second), BF),
    ]


class GradScatter(PlaneScatter):
    def __init__(self, ref, lands, send, recv, pair_land, pair_send, pair_recv):
        half = ref.shape[-1] // 2
        first, second = GRAD_HALF[ref.shape[-1]]
        core = lax.axis_index("section")
        low = pl.multiple_of(core * half, 128)
        super().__init__(ref, pl.ds(low, first), pl.ds(pl.multiple_of(low + first, 128), second), lands, send, recv)
        self.mine = pl.ds(low, half)
        self.theirs = pl.ds(pl.multiple_of((1 - core) * half, 128), half)
        self.pair_land = pair_land
        self.pair = remote(ref.at[:, :, :, self.theirs], pair_land, pair_send, pair_recv, section=1 - core)
        self.half, self.first = half, first

    def swap(self):
        self.pair.start()

    def start(self):
        self.pair.wait_recv()
        for row in range(EDGE):
            own = self.ref.at[row, :, :, self.mine]
            own[...] = (own[...].astype(F32) + self.pair_land[row].astype(F32)).astype(BF)
        super().start()

    def finish(self):
        self.pair.wait_send()
        super().finish()

    def result(self, out):
        a, b = self.end()
        out[:, self.a] = a
        out[:, self.b] = b


def weight_grad(ref, low, left_t, right):
    size = right.shape[1]
    for row in range(EDGE):
        block = mm(left_t[row * 256 : (row + 1) * 256], right)
        ref[row, :, :, low : low + size] = block.reshape(EDGE, BLOCK, size).astype(BF)


def turn_back(grads, values, gain, cos, sin):
    outs, terms = [], 0.0
    for index in range(values.shape[1] // HEAD_SIZE):
        grad = head(grads, index)
        grad = grad * cos + pltpu.roll(grad * sin, HEAD_SIZE // 2, 1)
        back, term = norm_back(head(values, index), grad, gain)
        outs.append(back.astype(BF))
        terms = terms + term
    return jnp.concatenate(outs, 1), terms


def wide(buf, low, size):
    return buf[:, :, :, low : low + size].reshape(-1, size)


BACK_IN = ("inputs", "cotangent")
BACK_KEPT = [(EDGE, EDGE, BLOCK, 1024), *[k[0][1:] for k in KEPT[1:]]]
SMALL = (8, WIDTH)
LANDS = [
    *scatter_lands(BLOCK, *GRAD_HALF[REST]), *scatter_lands(BLOCK, *GRAD_HALF[1024]), *scatter_lands(ROWS, 256, 256)
]


def backward_kernel(w1_all, w2_all, kv_all, *refs):
    names = (*BACK_IN, *STASH)
    st = dict(zip(names, refs))
    inner, inner_other, outs_other, g1_out, g2_out, small_out, *refs = refs[len(names) :]
    w1, w2, kv, dkv, g1, g2, res1, res2, pair1, pair2, part, landing, middle_grad, small, small_land, *refs = refs
    lands = [refs[n * len(LANDS) : (n + 1) * len(LANDS)] for n in range(2)]
    refs = refs[2 * len(LANDS) :]
    tp_sems, (load, send, recv, pair_send, pair_recv, small_send, small_recv, end_send, end_recv) = refs[:4], refs[4:]
    core = lax.axis_index("section")
    other = 1 - core
    here = lax.axis_index("tp")
    x, y = place()
    cos, sin, first = st["cos"][...], st["sin"][...], st["first"][...]
    sent = []
    loads = [
        [pltpu.make_async_copy(src, dst, load.at[layer, n])
         for n, (src, dst) in enumerate(
             ((w1_all.at[layer, :, :, :, 0:1024], w1), (w2_all.at[layer], w2), (kv_all.at[layer], kv)))]
        for layer in range(2)
    ]
    for n in (1, 2, 0):
        loads[1][n].start()
    greet_plane()
    rest = [
        GradScatter(g2.at[layer], lands[layer][0:4], send.at[layer, 0], recv.at[layer, 0],
                    pair2.at[layer], pair_send.at[layer, 0], pair_recv.at[layer, 0])
        for layer in range(2)
    ]
    head_grads = [
        GradScatter(g1, lands[layer][4:8], send.at[layer, 1], recv.at[layer, 1],
                    pair1.at[layer], pair_send.at[layer, 1], pair_recv.at[layer, 1])
        for layer in range(2)
    ]
    keys = [
        PlaneScatter(dkv, pl.ds(0, 256), pl.ds(256, 256), lands[layer][8:12], send.at[layer, 2], recv.at[layer, 2])
        for layer in range(2)
    ]
    small[...] = jnp.zeros(SMALL, F32)
    ends = [remote(st["outs"].at[other], outs_other, end_send.at[3], end_recv.at[3], section=other)]
    ends[0].start()
    rows = pl.ds(pl.multiple_of(here * SUB, SUB), SUB)
    def small_round(slot, peers):
        copies = []
        for n, where in enumerate(peers):
            copies.append(
                remote(small, small_land.at[slot + n], small_send.at[slot + n], small_recv.at[slot + n], **where)
            )
            copies[-1].start()
        return copies

    def small_add(slot, copies):
        for copy in copies:
            copy.wait()
        small[...] += sum(small_land[slot + n] for n in range(len(copies)))

    out_grad = st["cotangent"].at[core]
    for layer in (1, 0):
        hidden = st["outs"].at[0] if layer else st["inputs"].at[core]
        gains, head_gains = st["gains"][layer], st["head_gains"][layer]
        sems = [[s.at[2 * layer + n] for s in tp_sems] for n in range(2)]
        grad_low = out_grad[...]
        grad_rows = out_grad[rows, :].astype(F32)
        gate, up = st["gate"][layer], st["up"][layer]
        sigmoid = 1.0 / (1.0 + jnp.exp(-gate))
        loads[layer][1].wait()
        act_grad = mm(grad_low, wide(w2, DOWN, 768))
        gate_low = (act_grad * up * sigmoid * (1.0 + gate * (1.0 - sigmoid))).astype(BF)
        up_low = (act_grad * gate * sigmoid).astype(BF)
        activated = (gate * sigmoid * up).astype(BF)
        part[2 * layer] = (
            mm(gate_low, wide(w2, GATE, 768), (1, 1)) + mm(up_low, wide(w2, UP, 768), (1, 1))
        ).astype(BF)
        copies = tp_scatter(part.at[2 * layer], landing.at[2 * layer], *sems[0][:2])
        if layer == 0:
            rest[1].middle()
            head_grads[1].start()
        mlp_t = st["mlp_in"][layer].T
        weight_grad(g2.at[layer], GATE, mlp_t, gate_low)
        weight_grad(g2.at[layer], UP, mlp_t, up_low)
        total = tp_total(part.at[2 * layer], landing.at[2 * layer], copies)
        sent += copies
        back, terms = norm_back(st["after"][layer], total, gains[1:2])
        small[3 * layer + 1 : 3 * layer + 2, :] = terms
        grad_rows = grad_rows + back
        full = middle_grad.at[layer]
        tp_rows(full, here)[...] = grad_rows.astype(BF)
        sent += tp_spread(full, *sems[0][2:])
        weight_grad(g2.at[layer], DOWN, grad_low.T, activated)
        if layer == 0:
            rest[1].result(res2.at[1])
        tp_spread_wait(full, *sems[0][2:])
        grad_low = full[...]
        mixed_grad = mm(grad_low, wide(w2, OUT, 512)).astype(BF)
        if layer == 1:
            loads[0][1].start()
        weight_grad(g2.at[layer], OUT, grad_low.T, st["mixed"][layer])
        rest[layer].swap()
        loads[layer][2].wait()
        query = st["query"][layer]
        query_grads = []
        if layer == 0:
            head_grads[1].middle()
        for group in range(2):
            group_keys = wide(kv, group * HEAD_SIZE, HEAD_SIZE)
            group_values = wide(kv, 256 + group * HEAD_SIZE, HEAD_SIZE)
            keys_t = group_keys.T
            key_grad, value_grad = 0.0, 0.0
            for index in (2 * group, 2 * group + 1):
                head_query, head_grad = head(query, index), head(mixed_grad, index)
                scores = scores_t(group_keys, head_query, first)
                prob = jnp.exp(scores - st["level"][layer, index : index + 1, :])
                prob_grad = mm(group_values, head_grad, (1, 1))
                dots = jnp.sum(prob * prob_grad, 0, keepdims=True)
                score_low = (prob * (prob_grad - dots)).astype(BF)
                query_grads.append(mm(keys_t, score_low).T * SCALE)
                key_grad = key_grad + mm(score_low, head_query)
                value_grad = value_grad + mm(prob.astype(BF), head_grad)
            shape = (EDGE, EDGE, ROWS, HEAD_SIZE)
            dkv[:, :, :, group * HEAD_SIZE : (group + 1) * HEAD_SIZE] = (key_grad * SCALE).astype(BF).reshape(shape)
            low = 256 + group * HEAD_SIZE
            dkv[:, :, :, low : low + HEAD_SIZE] = value_grad.astype(BF).reshape(shape)
        keys[layer].start()
        if layer == 1:
            loads[0][2].start()
        query_low, terms = turn_back(
            jnp.concatenate(query_grads, 1), st["query_proj"][layer], head_gains[0:1], cos, sin
        )
        small[3 * layer + 2 : 3 * layer + 3, 0:128] = terms
        normed_t = st["normed"][layer].T
        if layer == 0:
            head_grads[1].result(res1.at[1])
            head_grads[1].finish()
        keys[layer].middle()
        rest[layer].start()
        weight_grad(g1, 0, normed_t, query_low)
        key_grad, value_grad = keys[layer].end()
        keys[layer].finish()
        key_low, terms = turn_back(key_grad, st["key_proj"][layer], head_gains[1:2], cos, sin)
        small[3 * layer + 2 : 3 * layer + 3, 128:256] = terms
        joined = jnp.concatenate([query_low, key_low, value_grad.astype(BF)], 1)
        loads[layer][0].wait()
        part[2 * layer + 1] = mm(joined, wide(w1, 0, 1024), (1, 1)).astype(BF)
        if layer == 1:
            loads[0][0].start()
        copies = tp_scatter(part.at[2 * layer + 1], landing.at[2 * layer + 1], *sems[1][:2])
        weight_grad(g1, 512, normed_t, joined[:, 512:])
        head_grads[layer].swap()
        total = tp_total(part.at[2 * layer + 1], landing.at[2 * layer + 1], copies)
        sent += copies
        back, terms = norm_back(hidden[rows, :].astype(F32), total, gains[0:1])
        small[3 * layer : 3 * layer + 1, :] = terms
        full = inner.at[layer]
        tp_rows(full, here)[...] = (grad_rows + back).astype(BF)
        sent += tp_spread(full, *sems[1][2:])
        if layer == 0:
            around_pair = small_round(0, [dict(section=other)])
            rest[0].middle()
            head_grads[0].start()
        tp_spread_wait(full, *sems[1][2:])
        out_grad = full
    ends.append(remote(inner.at[other], inner_other, end_send.at[0], end_recv.at[0], section=other))
    ends[1].start()

    steps = range(1, EDGE)

    def deliver(n, grad, res, out):
        grad.result(res.at[0])
        part_out = res.at[other, :, grad.mine]
        ends.append(remote(part_out, out.at[:, grad.mine], end_send.at[n], end_recv.at[n], section=other))
        ends[-1].start()
        out[:, grad.mine] = res[core, :, grad.mine]

    small_add(0, around_pair)
    around_x = small_round(1, [dict(ctx=peer_x(step)) for step in steps])
    head_grads[0].middle()
    small_add(1, around_x)
    around_y = small_round(4, [dict(ctx=peer_y(step)) for step in steps])
    deliver(2, rest[0], res2, g2_out)
    small_add(4, around_y)
    around_z = small_round(7, [dict(tp=ring("tp", step, TP)) for step in steps])
    deliver(1, head_grads[0], res1, g1_out)
    small_add(7, around_z)
    small_out[...] = small[...]
    ends[0].wait_recv()
    ends[1].wait_recv()
    for n, grad, out in ((2, rest[0], g2_out), (1, head_grads[0], g1_out)):
        dst = out.at[:, grad.theirs]
        remote(dst, dst, end_send.at[n], end_recv.at[n], section=core).wait_recv()
    finish(ends + sent)
    for grad in (*rest, head_grads[0]):
        grad.finish()


def run_backward(w1, w2, kv, *args):
    outs = [
        ((2, ROWS, WIDTH), BF), ((ROWS, WIDTH), BF), ((ROWS, WIDTH), BF), ((BLOCK, 1024), F32), ((BLOCK, REST), F32), (SMALL, F32),
    ]
    return pl.pallas_call(
        backward_kernel,
        out_shape=[jax.ShapeDtypeStruct(*o) for o in outs],
        in_specs=[HB] * 3 + [VM] * len(args),
        out_specs=[VM, HB, HB, VM, VM, VM],
        scratch_shapes=[
            *[pltpu.VMEM(k, BF) for k in BACK_KEPT],
            pltpu.VMEM((EDGE, EDGE, ROWS, 512), BF),
            pltpu.VMEM((EDGE, EDGE, BLOCK, 1024), BF),
            pltpu.VMEM((2, EDGE, EDGE, BLOCK, REST), BF),
            pltpu.VMEM((2, BLOCK, 1024), F32),
            pltpu.VMEM((2, BLOCK, REST), F32),
            pltpu.VMEM((2, EDGE, EDGE, BLOCK, 512), BF),
            pltpu.VMEM((2, EDGE, EDGE, BLOCK, REST // 2), BF),
            pltpu.VMEM((4, ROWS, WIDTH), BF),
            pltpu.VMEM((4, TP - 1, SUB, WIDTH), BF),
            pltpu.VMEM((2, ROWS, WIDTH), BF),
            pltpu.VMEM(SMALL, F32),
            pltpu.VMEM((10, *SMALL), F32),
            *[pltpu.VMEM(*k) for k in LANDS * 2],
            *[DMA((4, TP - 1))] * 4,
            DMA((2, 3)), DMA((2, 3, 12)), DMA((2, 3, 12)), DMA((2, 2)), DMA((2, 2)),
            DMA((10,)), DMA((10,)), DMA((4,)), DMA((4,)),
        ],
        compiler_params=params(2, 62),
    )(w1, w2, kv, *args)


def results_kernel(
    outs_all, outs_other_all, inner_all, inner_other_all, g1_all, g2_all, small_all, section_out, input_grad,
    attn_gain, query, key, value, query_gain, key_gain, output, mlp_gain, gate, up, down, *refs
):
    core, here = lax.axis_index("section"), lax.axis_index("ctx")
    loads = [
        pltpu.make_async_copy(src, dst, refs[-1].at[n])
        for n, (src, dst) in enumerate(
            zip(
                (outs_all.at[core], outs_other_all, inner_all.at[core], inner_other_all, g1_all, g2_all, small_all),
                refs[:-1],
            )
        )
    ]
    for load in loads:
        load.start()
    outs, outs_other, inner, inner_other, g1, g2, small = refs[:-1]
    for load in loads:
        load.wait()
    section_out[0, core] = outs[...]
    section_out[0, 1 - core] = outs_other[...]
    input_grad[0, core] = inner[...].astype(F32)
    input_grad[0, 1 - core] = inner_other[...].astype(F32)
    query[0] = g1[:, 0:512]
    key[0] = g1[:, 512:768]
    value[0] = g1[:, 768:1024]
    gate[0] = g2[:, GATE : GATE + 768]
    up[0] = g2[:, UP : UP + 768]
    output[0] = g2[:, OUT : OUT + 512]
    down[0] = g2[:, DOWN : DOWN + 768]
    for n, out in enumerate((attn_gain, mlp_gain)):
        row = small[pl.ds(3 * core + n, 1), :]
        own = jnp.zeros((1, BLOCK), F32)
        for index in range(CTX):
            own = jnp.where(here == index, row[:, index * BLOCK : (index + 1) * BLOCK], own)
        out[...] = own
    row = small[pl.ds(3 * core + 2, 1), :]
    query_gain[...] = row[:, 0:128]
    key_gain[...] = row[:, 128:256]


def on_device(
    inputs, positions, cotangent, attn_gain, w_query, w_key, w_value, query_gain, key_gain, w_output,
    mlp_gain, w_gate, w_up, w_down,
):
    w1, w2, kv, *stash = run_forward(
        inputs, positions, attn_gain, w_query, w_key, w_value, query_gain, key_gain,
        jnp.swapaxes(w_output, 1, 2), mlp_gain, w_gate, w_up, jnp.swapaxes(w_down, 1, 2),
    )
    inner, inner_other, outs_other, g1, g2, small = run_backward(w1, w2, kv, inputs, cotangent, *stash)
    outs = dict(zip(STASH, stash))["outs"]
    shapes = [
        ((1, 2, ROWS, WIDTH), BF), ((1, 2, ROWS, WIDTH), F32), ((1, BLOCK), F32), ((1, BLOCK, 512), F32),
        ((1, BLOCK, 256), F32), ((1, BLOCK, 256), F32), ((1, 128), F32), ((1, 128), F32), ((1, BLOCK, 512), F32),
        ((1, BLOCK), F32), ((1, BLOCK, 768), F32), ((1, BLOCK, 768), F32), ((1, BLOCK, 768), F32),
    ]
    results = list(pl.pallas_call(
        results_kernel,
        out_shape=[jax.ShapeDtypeStruct(*shape) for shape in shapes],
        in_specs=[HB] * 7,
        out_specs=[VM] * len(shapes),
        scratch_shapes=[
            *[pltpu.VMEM((ROWS, WIDTH), BF)] * 4,
            pltpu.VMEM((BLOCK, 1024), F32),
            pltpu.VMEM((BLOCK, REST), F32),
            pltpu.VMEM(SMALL, F32),
            DMA((7,)),
        ],
        compiler_params=pltpu.CompilerParams(vmem_limit_bytes=60 * 2**20),
    )(outs, outs_other, inner, inner_other, g1, g2, small))
    for n in (8, 12):
        results[n] = jnp.swapaxes(results[n], 1, 2)
    return tuple(results)


def solution(mesh):
    row, col = P("section", "ctx", "tp"), P("section", "tp", "ctx")
    gain, head = P("section", "ctx"), P("section", None)
    tokens = P(None, "ctx", None)
    layered = P("section", None, "ctx", None)
    return jax.shard_map(
        on_device,
        mesh=mesh,
        in_specs=(tokens, P(None, "ctx"), tokens, gain, row, row, row, head, head, col, gain, row, row, col),
        out_specs=(layered, layered, gain, row, row, row, head, head, col, gain, row, row, col),
        check_vma=False,
    )
```

profile of v0, /device:TPU:0, one launch (start us, length us, event | category | flops | bytes accessed | tf_op | source)
XLA Modules:
  0.0 277.1 jit_solution(11347236853152872432)
XLA Ops:
  0.6 136.2 %shard_map.246 = (bf16[2,4,4,64,1280]{4,3,2,1,0:T(8,128)(2,1)}, bf16[2,4,4,64,2816]{4,3,2,1,0:T(8,128)(2,1)}, bf16[2,4,4,128,512]{4,3,2,1,0:T(8,128)(2,1)}, s32[...) custom-call(bf16[2,128,1024]{2,1,0:T(8,128)(2,1)} %refs_0_.1, ...), custom_call_target="tpu_custom_call" | custom-call | tf_op jit(solution)/shard_map/pallas_call | solution.py:430
  136.8 136.9 %shard_map.247 = (bf16[2,128,1024]{2,1,0:T(8,128)(2,1)}, bf16[128,1024]{1,0:T(8,128)(2,1)}, bf16[128,1024]{1,0:T(8,128)(2,1)}, f32[64,1024]{1,0:T(8,128)}, f32[64,2816]{1,0:T(8,128)}, /*index=5*/f32[8,1024]{1,0:T(8,128)}) custom-call(bf16[2,4,4,64,1280]{4,3,2,1,0:T(8,128)(2,1)} %get-tuple-element.52.w1_all, ...), custom_call_target="tpu_custom_call" | custom-call | tf_op jit(solution)/shard_map/pallas_call | solution.py:821
  273.7 3.2 %shard_map.248 = (bf16[1,2,128,1024]{3,2,1,0:T(8,128)(2,1)}, f32[1,2,128,1024]{3,2,1,0:T(8,128)}, f32[1,64]{1,0:T(1,128)}, f32[1,64,512]{2,1,0:T(8,128)}, f32[1,...) custom-call(bf16[2,128,1024]{2,1,0:T(8,128)(2,1)} %get-tuple-element, ...), custom_call_target="tpu_custom_call" | custom-call | tf_op jit(solution)/shard_map/pallas_call | solution.py:905
where the time goes:
time: 282 us; the launch traced here: 277 us
  Pallas kernels  276 us (98%)
    pallas_call x1, Pallas kernels, run_backward(): pl.pallas_call(backward_kernel, out_shape=[jax.ShapeDtypeStruct(*o) for o...  137 us
    pallas_call x1, Pallas kernels, run_forward(): pl.pallas_call(forward_kernel, out_shape=[jax.ShapeDtypeStruct(*o) for o...  136 us

commit v1 on v0

--- a/solution.py
+++ b/solution.py
@@ -80,7 +80,10 @@
     pl.semaphore_signal(
         sem, inc=1, device_id={"section": 1 - lax.axis_index("section")}, device_id_type=MESH
     )
-    pl.semaphore_wait(sem, 3 * (EDGE - 1) + 1)
+
+
+def met_plane():
+    pl.semaphore_wait(pltpu.get_barrier_semaphore(), 3 * (EDGE - 1) + 1)
 
 
 class PlaneGather:
@@ -298,11 +301,12 @@
     up = mm(mlp_in[...], flat(w2, layer, UP, 768))
     st["gate"][layer] = gate
     st["up"][layer] = up
+    st["keep"](1, layer)
+    if following is None:
+        return sent
     activated = (gate / (1.0 + jnp.exp(-gate)) * up).astype(BF)
-    st["keep"](1, layer)
-    if following:
-        for group in following[1:]:
-            group.start()
+    for group in following[1:]:
+        group.start()
     part[2 * layer + 1] = mm(activated, flat(w2, layer, DOWN, 768), (1, 1)).astype(BF)
     sems = [s.at[2 * layer + 1] for s in tp_sems]
     copies = tp_scatter(part.at[2 * layer + 1], landing.at[2 * layer + 1], sems[0], sems[1])
@@ -310,8 +314,7 @@
     out = st["outs"].at[layer]
     out[rows, :] = (total + after).astype(BF)
     copies += tp_spread(out, sems[2], sems[3])
-    if following:
-        following[1].middle()
+    following[1].middle()
     tp_spread_wait(out, sems[2], sems[3])
     return sent + copies
 
@@ -330,7 +333,7 @@
     mlp_in=((2, ROWS, WIDTH), BF),
     gate=((2, ROWS, 768), F32),
     up=((2, ROWS, 768), F32),
-    outs=((2, ROWS, WIDTH), BF),
+    outs=((1, ROWS, WIDTH), BF),
     gains=((2, 8, WIDTH), F32),
     head_gains=((2, 8, HEAD_SIZE), F32),
 )
@@ -367,6 +370,7 @@
         ]
         for layer in range(2)
     ]
+    greet_plane()
     own1[:, 0:512] = w_query[0]
     own1[:, 512:768] = w_key[0]
     own1[:, 768:1024] = w_value[0]
@@ -378,7 +382,7 @@
     own2[:, UP : UP + 768] = w_up[0]
     own2[:, OUT : OUT + 512] = w_output[0]
     own2[:, DOWN : DOWN + 768] = w_down[0]
-    greet_plane()
+    met_plane()
     swaps, locals_ = [], []
     for n, (own, ref) in enumerate(((own1, w1), (own2, w2))):
         for low, width in [(g[1], g[2]) for g in GROUPS if g[0] == n]:
@@ -452,7 +456,7 @@
 
 def tp_scatter(part, landing, send, recv):
     copies = []
-    for step in range(1, TP):
+    for step in (2, 1, 3):
         peer = ring("tp", step, TP)
         copies.append(
             remote(tp_rows(part, peer), landing.at[step - 1], send.at[step - 1], recv.at[step - 1], tp=peer)
@@ -463,8 +467,9 @@
 
 def tp_total(part, landing, copies):
     total = tp_rows(part, lax.axis_index("tp"))[...].astype(F32)
-    for step, copy in enumerate(copies):
+    for copy in copies:
         copy.wait_recv()
+    for step in range(TP - 1):
         total = total + landing[step].astype(F32)
     return total
 
@@ -472,7 +477,7 @@
 def tp_spread(full, send, recv):
     here = lax.axis_index("tp")
     copies = []
-    for step in range(1, TP):
+    for step in (2, 1, 3):
         rows = tp_rows(full, here)
         copies.append(remote(rows, rows, send.at[step - 1], recv.at[step - 1], tp=ring("tp", step, TP)))
         copies[-1].start()
@@ -624,7 +629,7 @@
 def backward_kernel(w1_all, w2_all, kv_all, *refs):
     names = (*BACK_IN, *STASH)
     st = dict(zip(names, refs))
-    inner, inner_other, outs_other, g1_out, g2_out, small_out, *refs = refs[len(names) :]
+    inner, inner_other, outs, outs_other, g1_out, g2_out, small_out, *refs = refs[len(names) :]
     w1, w2, kv, dkv, g1, g2, res1, res2, pair1, pair2, part, landing, middle_grad, small, small_land, *refs = refs
     lands = [refs[n * len(LANDS) : (n + 1) * len(LANDS)] for n in range(2)]
     refs = refs[2 * len(LANDS) :]
@@ -641,9 +646,9 @@
              ((w1_all.at[layer, :, :, :, 0:1024], w1), (w2_all.at[layer], w2), (kv_all.at[layer], kv)))]
         for layer in range(2)
     ]
+    greet_plane()
     for n in (1, 2, 0):
         loads[1][n].start()
-    greet_plane()
     rest = [
         GradScatter(g2.at[layer], lands[layer][0:4], send.at[layer, 0], recv.at[layer, 0],
                     pair2.at[layer], pair_send.at[layer, 0], pair_recv.at[layer, 0])
@@ -659,8 +664,10 @@
         for layer in range(2)
     ]
     small[...] = jnp.zeros(SMALL, F32)
-    ends = [remote(st["outs"].at[other], outs_other, end_send.at[3], end_recv.at[3], section=other)]
-    ends[0].start()
+    met_plane()
+    outs[0] = st["outs"][0]
+    ends = [remote(outs.at[other], outs_other, end_send.at[3], end_recv.at[3], section=other)]
+    last_sems = [s.at[4] for s in tp_sems]
     rows = pl.ds(pl.multiple_of(here * SUB, SUB), SUB)
     def small_round(slot, peers):
         copies = []
@@ -697,6 +704,8 @@
         if layer == 0:
             rest[1].middle()
             head_grads[1].start()
+        else:
+            part[4] = mm(activated, wide(w2, DOWN, 768), (1, 1)).astype(BF)
         mlp_t = st["mlp_in"][layer].T
         weight_grad(g2.at[layer], GATE, mlp_t, gate_low)
         weight_grad(g2.at[layer], UP, mlp_t, up_low)
@@ -711,6 +720,8 @@
         weight_grad(g2.at[layer], DOWN, grad_low.T, activated)
         if layer == 0:
             rest[1].result(res2.at[1])
+        else:
+            last = tp_scatter(part.at[4], landing.at[4], *last_sems[:2])
         tp_spread_wait(full, *sems[0][2:])
         grad_low = full[...]
         mixed_grad = mm(grad_low, wide(w2, OUT, 512)).astype(BF)
@@ -718,6 +729,10 @@
             loads[0][1].start()
         weight_grad(g2.at[layer], OUT, grad_low.T, st["mixed"][layer])
         rest[layer].swap()
+        if layer == 1:
+            total = tp_total(part.at[4], landing.at[4], last)
+            outs[1, rows, :] = (total + st["after"][1]).astype(BF)
+            sent += last + tp_spread(outs.at[1], *last_sems[2:])
         loads[layer][2].wait()
         query = st["query"][layer]
         query_grads = []
@@ -745,6 +760,8 @@
         keys[layer].start()
         if layer == 1:
             loads[0][2].start()
+            tp_spread_wait(outs.at[1], *last_sems[2:])
+            ends[0].start()
         query_low, terms = turn_back(
             jnp.concatenate(query_grads, 1), st["query_proj"][layer], head_gains[0:1], cos, sin
         )
@@ -777,7 +794,6 @@
         sent += tp_spread(full, *sems[1][2:])
         if layer == 0:
             around_pair = small_round(0, [dict(section=other)])
-            rest[0].middle()
             head_grads[0].start()
         tp_spread_wait(full, *sems[1][2:])
         out_grad = full
@@ -795,12 +811,13 @@
 
     small_add(0, around_pair)
     around_x = small_round(1, [dict(ctx=peer_x(step)) for step in steps])
-    head_grads[0].middle()
+    rest[0].middle()
     small_add(1, around_x)
     around_y = small_round(4, [dict(ctx=peer_y(step)) for step in steps])
-    deliver(2, rest[0], res2, g2_out)
+    head_grads[0].middle()
     small_add(4, around_y)
     around_z = small_round(7, [dict(tp=ring("tp", step, TP)) for step in steps])
+    deliver(2, rest[0], res2, g2_out)
     deliver(1, head_grads[0], res1, g1_out)
     small_add(7, around_z)
     small_out[...] = small[...]
@@ -816,13 +833,13 @@
 
 def run_backward(w1, w2, kv, *args):
     outs = [
-        ((2, ROWS, WIDTH), BF), ((ROWS, WIDTH), BF), ((ROWS, WIDTH), BF), ((BLOCK, 1024), F32), ((BLOCK, REST), F32), (SMALL, F32),
+        ((2, ROWS, WIDTH), BF), ((ROWS, WIDTH), BF), ((2, ROWS, WIDTH), BF), ((ROWS, WIDTH), BF), ((BLOCK, 1024), F32), ((BLOCK, REST), F32), (SMALL, F32),
     ]
     return pl.pallas_call(
         backward_kernel,
         out_shape=[jax.ShapeDtypeStruct(*o) for o in outs],
         in_specs=[HB] * 3 + [VM] * len(args),
-        out_specs=[VM, HB, HB, VM, VM, VM],
+        out_specs=[VM, HB, VM, HB, VM, VM, VM],
         scratch_shapes=[
             *[pltpu.VMEM(k, BF) for k in BACK_KEPT],
             pltpu.VMEM((EDGE, EDGE, ROWS, 512), BF),
@@ -832,13 +849,13 @@
             pltpu.VMEM((2, BLOCK, REST), F32),
             pltpu.VMEM((2, EDGE, EDGE, BLOCK, 512), BF),
             pltpu.VMEM((2, EDGE, EDGE, BLOCK, REST // 2), BF),
-            pltpu.VMEM((4, ROWS, WIDTH), BF),
-            pltpu.VMEM((4, TP - 1, SUB, WIDTH), BF),
+            pltpu.VMEM((5, ROWS, WIDTH), BF),
+            pltpu.VMEM((5, TP - 1, SUB, WIDTH), BF),
             pltpu.VMEM((2, ROWS, WIDTH), BF),
             pltpu.VMEM(SMALL, F32),
             pltpu.VMEM((10, *SMALL), F32),
             *[pltpu.VMEM(*k) for k in LANDS * 2],
-            *[DMA((4, TP - 1))] * 4,
+            *[DMA((5, TP - 1))] * 4,
             DMA((2, 3)), DMA((2, 3, 12)), DMA((2, 3, 12)), DMA((2, 2)), DMA((2, 2)),
             DMA((10,)), DMA((10,)), DMA((4,)), DMA((4,)),
         ],
@@ -895,8 +912,7 @@
         inputs, positions, attn_gain, w_query, w_key, w_value, query_gain, key_gain,
         jnp.swapaxes(w_output, 1, 2), mlp_gain, w_gate, w_up, jnp.swapaxes(w_down, 1, 2),
     )
-    inner, inner_other, outs_other, g1, g2, small = run_backward(w1, w2, kv, inputs, cotangent, *stash)
-    outs = dict(zip(STASH, stash))["outs"]
+    inner, inner_other, outs, outs_other, g1, g2, small = run_backward(w1, w2, kv, inputs, cotangent, *stash)
     shapes = [
         ((1, 2, ROWS, WIDTH), BF), ((1, 2, ROWS, WIDTH), F32), ((1, BLOCK), F32), ((1, BLOCK, 512), F32),
         ((1, BLOCK, 256), F32), ((1, BLOCK, 256), F32), ((1, 128), F32), ((1, 128), F32), ((1, BLOCK, 512), F32),

time: 282 us -> 274 us (0.972)
  Pallas kernels: 276 us -> 269 us
    pallas_call x1, Pallas kernels: 136 us -> 125 us  [run_forward(): pl.pallas_call(forward_kernel, out_shape=[jax.ShapeDtypeStruct(*o) for o...]
    pallas_call x1, Pallas kernels: 137 us -> 140 us  [run_backward(): pl.pallas_call(backward_kernel, out_shape=[jax.ShapeDtypeStruct(*o) for o...]
where the time goes in v1:
time: 274 us; the launch traced here: 270 us
  Pallas kernels  269 us (98%)
    pallas_call x1, Pallas kernels, run_backward(): pl.pallas_call(backward_kernel, out_shape=[jax.ShapeDtypeStruct(*o) for o...  140 us
    pallas_call x1, Pallas kernels, run_forward(): pl.pallas_call(forward_kernel, out_shape=[jax.ShapeDtypeStruct(*o) for o...  125 us

profile of v1, /device:TPU:0, one launch (start us, length us, event | category | flops | bytes accessed | tf_op | source)
XLA Modules:
  0.0 269.5 jit_solution(10973620315562910626)
XLA Ops:
  0.6 125.4 %shard_map.246 = (bf16[2,4,4,64,1280]{4,3,2,1,0:T(8,128)(2,1)}, bf16[2,4,4,64,2816]{4,3,2,1,0:T(8,128)(2,1)}, bf16[2,4,4,128,512]{4,3,2,1,0:T(8,128)(2,1)}, s32[...) custom-call(bf16[2,128,1024]{2,1,0:T(8,128)(2,1)} %refs_0_.1, ...), custom_call_target="tpu_custom_call" | custom-call | tf_op jit(solution)/shard_map/pallas_call | solution.py:434
  126.0 140.1 %shard_map.247 = (bf16[2,128,1024]{2,1,0:T(8,128)(2,1)}, bf16[128,1024]{1,0:T(8,128)(2,1)}, bf16[2,128,1024]{2,1,0:T(8,128)(2,1)}, bf16[128,1024]{1,0:T(8,128)(2...) custom-call(bf16[2,4,4,64,1280]{4,3,2,1,0:T(8,128)(2,1)} %get-tuple-element.52.w1_all, ...), custom_call_target="tpu_custom_call" | custom-call | tf_op jit(solution)/shard_map/pallas_call | solution.py:838
  266.2 3.2 %shard_map.248 = (bf16[1,2,128,1024]{3,2,1,0:T(8,128)(2,1)}, f32[1,2,128,1024]{3,2,1,0:T(8,128)}, f32[1,64]{1,0:T(1,128)}, f32[1,64,512]{2,1,0:T(8,128)}, f32[1,...) custom-call(bf16[2,128,1024]{2,1,0:T(8,128)(2,1)} %get-tuple-element, ...), custom_call_target="tpu_custom_call" | custom-call | tf_op jit(solution)/shard_map/pallas_call | solution.py:921
